TPU v7x, 512 devices: a whole 4x8x8 slice. The times are simulated.
512 devices in a mesh: dp: 32 (over z, y_hi), segment: 2 (over y_lo), mp: 8 (over x, core).
Axes of the slice: x: 4, y: 8 (y_hi: 4, y_lo: 2; y = y_hi * 2 + y_lo), z: 8, core: 2. Of those that a mesh axis runs over, the one named last changes fastest.
Arguments:
- prefix_hidden: bfloat16 [64, 512, 8192], P(('dp', 'segment'), 'mp'), may hold values from -16 to 16
- norm_gain: float32 [8192], replicated, may hold values from 0.5 to 1.5
- kv_weight: bfloat16 [8192, 2, 1024], P('dp', None, 'mp'), may hold values from -0.0625 to 0.0625
- action_query: bfloat16 [64, 128, 2048], P(('dp', 'segment'), None, 'mp'), may hold values from -104 to 104
- action_kv: bfloat16 [64, 128, 2, 1024], P(('dp', 'segment'), None, None, 'mp'), may hold values from -4.25 to 4.25
- out_cotangent: bfloat16 [64, 128, 2048], P(('dp', 'segment'), None, 'mp'), may hold values from -18 to 18
- prefix_blocks: int32 [64, 512], P(('dp', 'segment')), may hold values from 0 to 7, as said below
- action_blocks: int32 [64, 128], P(('dp', 'segment')), may hold values from 0 to 8, as said below
- prefix_lengths: int32 [64], P(('dp', 'segment')), may hold values from 128 to 512, as said below
- timesteps: int32 [64], P(('dp', 'segment')), may hold values from 0 to 999
Outputs:
- attn_out: bfloat16 [64, 128, 2048], P(('dp', 'segment'), None, 'mp')
- query_grad: float32 [64, 128, 2048], P(('dp', 'segment'), None, 'mp')
- action_kv_grad: float32 [64, 128, 2, 1024], P(('dp', 'segment'), None, None, 'mp')
- weight_grad: float32 [8192, 2, 1024], P('dp', None, 'mp')
Inputs may be any that keep to these rules, and one draw needn't show every extreme that they name: `prefix_blocks`: constant over each run of 64 positions, 0 on the first run, rising by 0 or 1 from one run to the next; in every draw some sample rises at every run. `action_blocks`: constant over each run of 64 positions; the last run of every sample holds 8; in every draw some sample's first run holds 0. `prefix_lengths`: in every draw some sample's prefix is whole and some sample's is 128.
All inputs are finite; a program needn't handle non-finite values.
Results may differ from a plain program's by a relative error of at most 0.017.
Values may be sent and summed in bfloat16 or wider, within the bound.
No kernel may reach another device: no remote copies, remote signals or barrier semaphores. Data moves between devices by JAX's collectives and lax.ppermute only.
A program may use at most 64 MiB of HBM per device.

v0:
```python
import jax
import jax.numpy as jnp
from jax import lax
from jax.sharding import Mesh
from jax.sharding import PartitionSpec as P

KVH = 8
HD = 128
QH = 16
STEPS = 1000
DP = ("dp_0", "dp_1")
DP_SEGMENT = ("dp_0", "dp_1", "segment")
EPS = 1e-06
NEGATIVE = -1e30


def sum_by_axis(terms, axes):
    subtotal = terms.astype(jnp.bfloat16)
    for axis in axes:
        subtotal = lax.psum_scatter(subtotal, axis, scatter_dimension=0, tiled=True)
    return subtotal.astype(jnp.float32)


def from_everyone(array, axis):
    copies = jnp.broadcast_to(array, (lax.axis_size(axis), *array.shape))
    return lax.all_to_all(copies, axis, split_axis=0, concat_axis=0, tiled=True)


def taken_together(array, axis):
    everything = from_everyone(array, axis)
    return jnp.sum(everything.astype(jnp.float32), axis=0)


def head_scores(query, keys):
    return jnp.einsum("agrh,jgh->graj", query, keys, preferred_element_type=jnp.float32) * HD ** (
        -0.5
    )


def backward_terms(probs, values, keys, query, grad_out):
    probs_low = probs.astype(jnp.bfloat16)
    d_probs = jnp.einsum("agrh,jgh->graj", grad_out, values, preferred_element_type=jnp.float32)
    delta = jnp.sum(probs * d_probs, axis=-1, keepdims=True)
    d_scores = (probs * (d_probs - delta)).astype(jnp.bfloat16)
    d_query = jnp.einsum(
        "graj,jgh->agrh", d_scores, keys, preferred_element_type=jnp.float32
    ) * HD ** (-0.5)
    d_keys = jnp.einsum(
        "graj,agrh->jgh", d_scores, query, preferred_element_type=jnp.float32
    ) * HD ** (-0.5)
    d_values = jnp.einsum("graj,agrh->jgh", probs_low, grad_out, preferred_element_type=jnp.float32)
    return (d_query, jnp.stack([d_keys, d_values], axis=1))


def shards(
    prefix_hidden,
    norm_gain,
    kv_weight,
    action_query,
    action_kv,
    out_cotangent,
    prefix_blocks,
    action_blocks,
    prefix_lengths,
    timesteps,
):
    acts = action_query.shape[1]
    heads_kv = kv_weight.shape[2] // HD
    ratio = QH // KVH
    columns = 2 * kv_weight.shape[2]
    wide = prefix_hidden[0].astype(jnp.float32)
    inverse = lax.rsqrt(jnp.mean(wide * wide, axis=-1, keepdims=True) + EPS)
    normed_local = (wide * inverse * norm_gain).astype(jnp.bfloat16)
    normed = lax.all_gather(normed_local, "mp", axis=0, tiled=True)
    rows = normed.shape[0]
    piece = lax.all_gather(kv_weight, DP, axis=0, tiled=True)
    section = normed
    projected = jnp.dot(
        section, piece.reshape(piece.shape[0], columns), preferred_element_type=jnp.float32
    )
    prefix_kv = projected.astype(jnp.bfloat16).reshape(rows, 2, heads_kv, HD)
    own_pair = action_kv[0].reshape(acts, 2, heads_kv, HD)
    query = action_query[0].reshape(acts, heads_kv, ratio, HD)
    flow_weight = 0.5 + (timesteps[0].astype(jnp.float32) + 0.5) / STEPS
    grad_out = (
        (flow_weight * out_cotangent[0].astype(jnp.float32))
        .astype(jnp.bfloat16)
        .reshape(acts, heads_kv, ratio, HD)
    )
    pblocks = prefix_blocks[0]
    ablocks = action_blocks[0]
    length = prefix_lengths[0]
    keys = jnp.concatenate([prefix_kv[:, 0], own_pair[:, 0]], axis=0)
    values = jnp.concatenate([prefix_kv[:, 1], own_pair[:, 1]], axis=0)
    positions = jnp.arange(rows, dtype=jnp.int32)
    see_prefix = (pblocks[None, :] <= ablocks[:, None]) & (positions[None, :] < length)
    see_action = ablocks[None, :] <= ablocks[:, None]
    visible = jnp.concatenate([see_prefix, see_action], axis=1)
    masked = jnp.where(visible, head_scores(query, keys), NEGATIVE)
    top = jnp.max(masked, axis=-1, keepdims=True)
    expo = jnp.where(visible, jnp.exp(masked - top), 0.0)
    probs = expo / jnp.sum(expo, axis=-1, keepdims=True)
    out = jnp.einsum(
        "graj,jgh->agrh", probs.astype(jnp.bfloat16), values, preferred_element_type=jnp.float32
    )
    d_query, d_pair = backward_terms(probs, values, keys, query, grad_out)
    d_prefix = d_pair[:rows]
    d_action = d_pair[rows:]
    attn_out = out.astype(jnp.bfloat16).reshape(1, acts, ratio * heads_kv * HD)
    query_grad = d_query.reshape(1, acts, ratio * heads_kv * HD)
    action_kv_grad = d_action.reshape(1, acts, 2, heads_kv * HD)
    prefix_grad = d_prefix.astype(jnp.bfloat16).reshape(rows, columns)
    section = normed
    term = lax.dot_general(
        section, prefix_grad, (((0,), (0,)), ((), ())), preferred_element_type=jnp.float32
    )
    shard = sum_by_axis(term.reshape(kv_weight.shape[0] * lax.axis_size(DP), 2, columns // 2), DP)
    weight_grad = taken_together(shard.astype(jnp.bfloat16), "segment").astype(jnp.float32)
    return (attn_out, query_grad, action_kv_grad, weight_grad)


def solution(mesh):
    torus = Mesh(
        mesh.devices.reshape(8, 4, mesh.shape["segment"], mesh.shape["mp"]),
        ("dp_0", "dp_1", "segment", "mp"),
    )
    placed = (
        P(DP_SEGMENT, "mp", None),
        P(),
        P(DP, None, "mp"),
        P(DP_SEGMENT, None, "mp"),
        P(DP_SEGMENT, None, None, "mp"),
        P(DP_SEGMENT, None, "mp"),
        P(DP_SEGMENT, None),
        P(DP_SEGMENT, None),
        P(DP_SEGMENT),
        P(DP_SEGMENT),
    )
    return jax.shard_map(
        shards,
        mesh=torus,
        in_specs=placed,
        out_specs=(
            P(DP_SEGMENT, None, "mp"),
            P(DP_SEGMENT, None, "mp"),
            P(DP_SEGMENT, None, None, "mp"),
            P(DP, None, "mp"),
        ),
        check_vma=False,
    )
```

profile of v0, /device:TPU:18, one launch (start us, length us, event | category | flops | bytes accessed | tf_op | source)
XLA Modules:
  0.0 294.3 jit_solution(14425961718619464857)
XLA Ops:
  7.2 0.0 copy-start
  7.2 0.0 copy-start.1
  7.2 0.0 copy-start.2
  7.2 0.0 copy-start.3
  7.2 0.0 copy-start.4
  7.2 0.0 all-gather.5.cloned.1.call-start
  7.3 0.7 all-gather.5.cloned.1.call-update
  8.0 0.0 all-gather.3.cloned.1.call-start
  8.0 1.5 fusion.4
  9.5 2.6 fusion.6
  12.1 0.0 all-gather.3.cloned.1.call-update
  12.2 0.0 reduce-scatter.3.cloned.1.call-start
  12.2 0.0 copy-done
  12.2 0.1 copy.52
  12.4 0.0 copy-done.1
  12.4 0.1 copy.77
  13.8 0.0 copy-done.2
  13.8 0.1 copy.78
  14.0 0.0 copy-done.3
  14.0 0.1 broadcast_compare_fusion
  14.1 0.0 copy-done.4
  14.1 0.2 compare_and_fusion
  14.3 102.6 %all-gather.5.cloned.1.call-done = bf16[8192,2,128]{2,1,0:T(2,128)(2,1)} async-done(((bf16[256,2,128]{2,1,0:T(2,128)(2,1)}), bf16[8192,2,128]{2,1,0:T(2,128)(2,1)}) %all-gather.5.cloned.1.call-update) | async-done | bytes 4194320 | tf_op jit(solution)/shard_map/all_gather | solution.py:76
  116.9 54.1 %all-gather.3.cloned.1.call-done = bf16[512,8192]{1,0:T(8,128)(2,1)} async-done(((bf16[64,8192]{1,0:T(8,128)(2,1)}), bf16[512,8192]{1,0:T(8,128)(2,1)}) %all-gather.3.cloned.1.call-update) | async-done | bytes 8388624 | tf_op jit(solution)/shard_map/all_gather | solution.py:74
  170.9 6.9 %fusion.8 = bf16[512,256]{0,1:T(8,128)(2,1)S(1)} fusion(bf16[512,8192]{1,0:T(8,128)(2,1)} %all-gather.3.cloned.1.call-done, bf16[1024,8,2,128]{3,2,1,0:T(2,128)(2,1)} %bitcast.129), kind=kOutput, calls=%fused_computation.13 | convolution fusion | flops 2147614720 | bytes 12845056 | tf_op jit(solution)/shard_map/dot_general | solution.py:78
  177.9 0.1 copy.76
  178.0 0.3 fusion.33
  178.3 0.1 fusion.15
  178.5 0.3 convolution_bitcast_fusion.1
  178.8 0.3 multiply_reduce_fusion
  179.1 0.2 fusion.17
  179.3 0.2 fusion.13
  179.6 2.3 copy-done.5
  181.8 4.0 %convolution_convert_fusion = bf16[8192,2,128]{2,0,1:T(8,128)(2,1)} fusion(bf16[512,8192]{1,0:T(8,128)(2,1)S(1)} %copy-done.5, f32[640,1,1,128]{0,3,2,1:T(8,128)S(1)} %convolution_bitcast_fusion.1, f32[640,1,1,128]{0,3,2,1:T(8,128)S(1)} %fusion.13), kind=kOutput, calls=%fused_computation | convolution fusion | flops 2150105088 | bytes 13238272 | tf_op jit(solution)/shard_map/dot_general | solution.py:114
  185.8 0.0 reduce-scatter.3.cloned.1.call-update
  185.8 0.0 reduce-scatter.5.cloned.1.call-start
  185.9 59.9 %reduce-scatter.3.cloned.1.call-done = bf16[1024,2,128]{2,0,1:T(8,128)(2,1)} async-done(((bf16[8192,2,128]{2,0,1:T(8,128)(2,1)}), bf16[1024,2,128]{2,0,1:T(8,128)(2,1)}) %reduce-scatter.3.cloned.1.call-update) | async-done | bytes 524304 | tf_op jit(solution)/shard_map/reduce_scatter | solution.py:20
  245.7 0.0 reduce-scatter.5.cloned.1.call-update
  245.8 0.3 convolution_convert_fusion.1
  246.1 0.7 copy.64
  246.8 29.7 %reduce-scatter.5.cloned.1.call-done = bf16[256,2,128]{2,0,1:T(8,128)(2,1)} async-done(((bf16[1024,2,128]{2,0,1:T(8,128)(2,1)}), bf16[256,2,128]{2,0,1:T(8,128)(2,1)}) %reduce-scatter.5.cloned.1.call-update) | async-done | bytes 131088 | tf_op jit(solution)/shard_map/reduce_scatter | solution.py:20
  276.6 1.6 broadcast_in_dim.24
  278.2 3.4 %all-to-all-start = ((bf16[2,256,2,128]{3,1,2,0:T(8,128)(2,1)}), bf16[2,256,2,128]{3,1,2,0:T(8,128)(2,1)S(1)}, u32[]{:S(2)}, u32[]{:S(2)}) async-start(bf16[2,256,2,128]{3,1,2,0:T(8,128)(2,1)} %broadcast_in_dim.24), calls=%async_computation.2 | async-start | bytes 524288 | tf_op jit(solution)/shard_map/all_to_all | solution.py:26
  281.7 0.3 convolution_multiply_fusion.1
  281.9 0.8 copy.65
  282.7 0.8 copy.66
  283.4 3.4 %all-to-all-done = bf16[2,256,2,128]{3,1,2,0:T(8,128)(2,1)S(1)} async-done(((bf16[2,256,2,128]{3,1,2,0:T(8,128)(2,1)}), bf16[2,256,2,128]{3,1,2,0:T(8,128)(2,1)S(1)}, u32[]{:S(2)}, u32[]{:S(2)}) %all-to-all-start) | async-done | bytes 262176 | tf_op jit(solution)/shard_map/all_to_all | solution.py:26
  286.8 0.9 copy.67
  (11 shorter events, 0.1 us)
Async XLA Ops:
  7.2 5.0 %copy-start = (bf16[1,128,2,128]{3,2,1,0:T(2,128)(2,1)S(1)}, bf16[1,128,2,128]{3,2,1,0:T(2,128)(2,1)}, u32[]{:S(2)}) copy-start(bf16[1,128,2,128]{3,2,1,0:T(2,128)(2,1)} %param.14) | copy-start | bytes 196612
  7.2 5.2 %copy-start.1 = (bf16[1,128,256]{2,1,0:T(8,128)(2,1)S(1)}, bf16[1,128,256]{2,1,0:T(8,128)(2,1)}, u32[]{:S(2)}) copy-start(bf16[1,128,256]{2,1,0:T(8,128)(2,1)} %param.13) | copy-start | bytes 196612
  7.2 6.6 %copy-start.2 = (bf16[1,128,256]{2,1,0:T(8,128)(2,1)S(1)}, bf16[1,128,256]{2,1,0:T(8,128)(2,1)}, u32[]{:S(2)}) copy-start(bf16[1,128,256]{2,1,0:T(8,128)(2,1)} %param.15) | copy-start | bytes 196612
  7.2 6.8 %copy-start.3 = (s32[1,128]{1,0:T(1,128)S(1)}, s32[1,128]{1,0:T(1,128)}, u32[]{:S(2)}) copy-start(s32[1,128]{1,0:T(1,128)} %param.17) | copy-start | bytes 1540
  7.2 6.9 %copy-start.4 = (s32[1,512]{1,0:T(1,128)S(1)}, s32[1,512]{1,0:T(1,128)}, u32[]{:S(2)}) copy-start(s32[1,512]{1,0:T(1,128)} %param.16) | copy-start | bytes 6148
  7.2 109.6 %all-gather.5.cloned.1.call-start = ((), (), s32[]{:S(2)}) async-start(), calls=%async_computation.4 | async-start | bytes 4325376 | tf_op jit(solution)/shard_map/all_gather | solution.py:76
  8.0 163.0 %all-gather.3.cloned.1.call-start = ((), (), s32[]{:S(2)}) async-start(), calls=%async_computation.3 | async-start | bytes 9437184 | tf_op jit(solution)/shard_map/all_gather | solution.py:74
  12.2 233.6 %reduce-scatter.3.cloned.1.call-start = ((), (), s32[]{:S(2)}) async-start(), calls=%async_computation.5 | async-start | bytes 4718592 | tf_op jit(solution)/shard_map/reduce_scatter | solution.py:20
  178.5 3.4 %copy-start.5 = (bf16[512,8192]{1,0:T(8,128)(2,1)S(1)}, bf16[512,8192]{1,0:T(8,128)(2,1)}, u32[]{:S(2)}) copy-start(bf16[512,8192]{1,0:T(8,128)(2,1)} %all-gather.3.cloned.1.call-done) | copy-start | bytes 25165828
  185.8 90.7 %reduce-scatter.5.cloned.1.call-start = ((), (), s32[]{:S(2)}) async-start(), calls=%async_computation.6 | async-start | bytes 655360 | tf_op jit(solution)/shard_map/reduce_scatter | solution.py:20
  278.2 8.6 %all-to-all-start = ((bf16[2,256,2,128]{3,1,2,0:T(8,128)(2,1)}), bf16[2,256,2,128]{3,1,2,0:T(8,128)(2,1)S(1)}, u32[]{:S(2)}, u32[]{:S(2)}) async-start(bf16[2,256,2,128]{3,1,2,0:T(8,128)(2,1)} %broadcast_in_dim.24), calls=%async_computation.2 | async-start | bytes 524288 | tf_op jit(solution)/shard_map/all_to_all | solution.py:26
Sparse Core Ops, SparseCore 0:
  11.2 105.6 all-gather.4
  119.0 51.8 all-gather.2
  185.9 59.7 reduce-scatter.2
  248.4 28.1 reduce-scatter.4
where the time goes:
time: 295 us; the launch traced here: 294 us
  waiting for transfers between devices  250 us (85%)
  between operations  15.3 us (5%)
  matrix products  12.6 us (4%)
  local copies, waits for them, and re-layouts  7.58 us (3%)
  other arithmetic  4.84 us (2%)
  starting transfers between devices  3.6 us (1%)
    all_gather x1, waiting for transfers between devices, shards(): piece = lax.all_gather(kv_weight, DP, axis=0, tiled=True)  103 us
    reduce_scatter x2, waiting for transfers between devices, sum_by_axis(): subtotal = lax.psum_scatter(subtotal, axis, scatter_dimension=0, tiled=True)  89.6 us
    all_gather x1, waiting for transfers between devices, shards(): normed = lax.all_gather(normed_local, 'mp', axis=0, tiled=True)  54.1 us
    dot_general x1, matrix products, shards(): jnp.dot(section, piece.reshape(piece.shape[0], columns), preferred_elemen...  6.94 us
  transfers between devices with their start and end apart: 5, of which 5 were waited for; matrix products, arithmetic and copies ran while one was open for 3% of the time, Pallas kernels for 0%

commit v1 on v0

--- a/solution.py
+++ b/solution.py
@@ -12,6 +12,22 @@
 DP_SEGMENT = ("dp_0", "dp_1", "segment")
 EPS = 1e-06
 NEGATIVE = -1e30
+
+
+def close_core(out_dim, piece_in):
+    n = lax.axis_size("mp")
+    frames = tuple(((dev_j, (dev_j + 1) % n) for dev_j in range(n)))
+    found = tuple(((dev_j, (dev_j - 1) % n) for dev_j in range(n)))
+    shaped, then = ([piece_in], [piece_in])
+    for _ in range(n // 2):
+        part_next = lax.ppermute(shaped[-1], "mp", frames)
+        shaped.append(part_next)
+    for _ in range((n - 1) // 2):
+        piece_next = lax.ppermute(then[-1], "mp", found)
+        then.append(piece_next)
+    raw_out = jnp.concatenate([*shaped[::-1], *then[1:]], axis=out_dim)
+    u_next = lax.axis_index("mp")
+    return jnp.roll(raw_out, (u_next - n // 2) * piece_in.shape[out_dim], axis=out_dim)
 
 
 def sum_by_axis(terms, axes):
@@ -71,7 +87,7 @@
     wide = prefix_hidden[0].astype(jnp.float32)
     inverse = lax.rsqrt(jnp.mean(wide * wide, axis=-1, keepdims=True) + EPS)
     normed_local = (wide * inverse * norm_gain).astype(jnp.bfloat16)
-    normed = lax.all_gather(normed_local, "mp", axis=0, tiled=True)
+    normed = close_core(0, normed_local)
     rows = normed.shape[0]
     piece = lax.all_gather(kv_weight, DP, axis=0, tiled=True)
     section = normed

time: 295 us -> 259 us (0.88)
  waiting for transfers between devices: 250 us -> 137 us
  local copies, waits for them, and re-layouts: 7.58 us -> 65.1 us
  matrix products: 12.6 us -> 22.3 us
  starting transfers between devices: 3.6 us -> 9.21 us
    all_gather x1, waiting for transfers between devices: 103 us -> 0.02 us  [shards(): piece = lax.all_gather(kv_weight, DP, axis=0, tiled=True)]
    all_gather x1 -> x0, waiting for transfers between devices: 54.1 us -> none  [shards(): normed = lax.all_gather(normed_local, 'mp', axis=0, tiled=True)]
    concatenate x0 -> x1, local copies, waits for them, and re-layouts: none -> 37.6 us  [close_core(): jnp.roll(raw_out, (u_next - n // 2) * piece_in.shape[out_dim], axis=out_dim)]
    ppermute x0 -> x7, waiting for transfers between devices: none -> 36.2 us  [the longest x4 36.2 us: close_core(): part_next = lax.ppermute(shaped[-1], 'mp', frames)]
    ppermute x0 -> x7, local copies, waits for them, and re-layouts: none -> 18.2 us  [the longest x4 10 us: close_core(): part_next = lax.ppermute(shaped[-1], 'mp', frames)]
    reduce_scatter x2, waiting for transfers between devices: 89.6 us -> 97.6 us  [sum_by_axis(): subtotal = lax.psum_scatter(subtotal, axis, scatter_dimension=0, tiled=True)]
    dot_general x1, matrix products: 3.96 us -> 11.1 us  [shards(): lax.dot_general(section, prefix_grad, (((0,), (0,)), ((), ())), preferred...]
    ppermute x0 -> x7, starting transfers between devices: none -> 5.65 us  [the longest x3 5.64 us: close_core(): piece_next = lax.ppermute(then[-1], 'mp', found)]
  transfers between devices with their start and end apart: 5 -> 11, of which waited for: 5 -> 6; matrix products, arithmetic and copies ran while one was open for 3% -> 27% of each run, Pallas kernels for 0% -> 0%
where the time goes in v1:
time: 259 us; the launch traced here: 256 us
  waiting for transfers between devices  137 us (53%)
  local copies, waits for them, and re-layouts  65.1 us (25%)
  matrix products  22.3 us (9%)
  between operations  15.3 us (6%)
  starting transfers between devices  9.21 us (4%)
  other arithmetic  6.46 us (2%)
    reduce_scatter x2, waiting for transfers between devices, sum_by_axis(): subtotal = lax.psum_scatter(subtotal, axis, scatter_dimension=0, tiled=True)  97.6 us
    concatenate x1, local copies, waits for them, and re-layouts, close_core(): jnp.roll(raw_out, (u_next - n // 2) * piece_in.shape[out_dim], axis=out_dim)  37.6 us
    ppermute x4, waiting for transfers between devices, close_core(): part_next = lax.ppermute(shaped[-1], 'mp', frames)  36.2 us
    dot_general x1, matrix products, shards(): lax.dot_general(section, prefix_grad, (((0,), (0,)), ((), ())), preferred...  11.1 us
    ppermute x4, local copies, waits for them, and re-layouts, close_core(): part_next = lax.ppermute(shaped[-1], 'mp', frames)  10 us
    dot_general x1, matrix products, shards(): jnp.dot(section, piece.reshape(piece.shape[0], columns), preferred_elemen...  9.54 us
    ppermute x3, local copies, waits for them, and re-layouts, close_core(): piece_next = lax.ppermute(then[-1], 'mp', found)  8.2 us
    ppermute x3, starting transfers between devices, close_core(): piece_next = lax.ppermute(then[-1], 'mp', found)  5.64 us
  transfers between devices with their start and end apart: 11, of which 6 were waited for; matrix products, arithmetic and copies ran while one was open for 27% of the time, Pallas kernels for 0%

profile of v1, /device:TPU:18, one launch (start us, length us, event | category | flops | bytes accessed | tf_op | source)
XLA Modules:
  0.0 255.5 jit_solution(14901001172727015877)
XLA Ops:
  7.2 0.0 all-gather.2.cloned.1.call-start
  7.2 0.7 all-gather.2.cloned.1.call-update
  7.9 0.0 reduce-scatter.3.cloned.1.call-start
  8.0 2.0 copy.68
  10.0 1.1 fusion.4
  11.1 0.2 copy-done
  11.4 4.7 %fusion.6 = bf16[64,8192]{0,1:T(8,128)(2,1)S(1)} fusion(bf16[1,64,8192]{1,2,0:T(8,128)(2,1)} %copy-done, f32[8192]{0:T(1024)S(1)} %copy-done.4, f32[64]{0:T(128)S(1)} %add_rsqrt_fusion), kind=kLoop, calls=%fused_computation.9 | loop fusion | flops 2097152 | bytes 2130176 | tf_op jit(solution)/shard_map/convert_element_type | solution.py:89
  16.0 1.6 copy.69
  17.7 1.7 collective-permute-start.4
  19.4 12.7 %collective-permute-done = bf16[64,8192]{1,0:T(8,128)(2,1)S(1)} collective-permute-done((bf16[64,8192]{1,0:T(8,128)(2,1)}, bf16[64,8192]{1,0:T(8,128)(2,1)S(1)}, u32[]{:S(2)}, u32[]{:S(2)}) %collective-permute-start) | collective-permute-done | bytes 1048608 | tf_op jit(solution)/shard_map/ppermute | solution.py:23
  32.1 2.1 collective-permute-start.5
  34.3 12.2 %collective-permute-done.1 = bf16[64,8192]{1,0:T(8,128)(2,1)} collective-permute-done((bf16[64,8192]{1,0:T(8,128)(2,1)S(1)}, bf16[64,8192]{1,0:T(8,128)(2,1)}, u32[]{:S(2)}, u32[]{:S(2)}) %collective-permute-start.1) | collective-permute-done | bytes 1048608 | tf_op jit(solution)/shard_map/ppermute | solution.py:23
  47.1 0.1 copy.112
  47.9 1.8 collective-permute-start.6
  49.7 11.3 %collective-permute-done.2 = bf16[64,8192]{1,0:T(8,128)(2,1)} collective-permute-done((bf16[64,8192]{1,0:T(8,128)(2,1)}, bf16[64,8192]{1,0:T(8,128)(2,1)}, u32[]{:S(2)}, u32[]{:S(2)}) %collective-permute-start.2) | collective-permute-done | bytes 1048608 | tf_op jit(solution)/shard_map/ppermute | solution.py:23
  61.0 0.1 copy.113
  61.2 0.1 copy.87
  61.3 0.1 broadcast_compare_fusion
  61.4 0.2 compare_and_fusion
  61.6 1.8 copy.74
  63.4 2.7 %copy.75 = bf16[64,8192]{0,1:T(8,128)(2,1)} copy(bf16[64,8192]{1,0:T(8,128)(2,1)} %collective-permute-done.4) | data formatting | bytes 2097152 | tf_op jit(solution)/shard_map/ppermute | solution.py:26
  66.2 2.7 %copy.73 = bf16[64,8192]{0,1:T(8,128)(2,1)} copy(bf16[64,8192]{1,0:T(8,128)(2,1)} %collective-permute-done.1) | data formatting | bytes 2097152 | tf_op jit(solution)/shard_map/ppermute | solution.py:23
  68.9 2.7 %copy.76 = bf16[64,8192]{0,1:T(8,128)(2,1)} copy(bf16[64,8192]{1,0:T(8,128)(2,1)} %collective-permute-done.5) | data formatting | bytes 2097152 | tf_op jit(solution)/shard_map/ppermute | solution.py:26
  71.6 2.7 %copy.72 = bf16[64,8192]{0,1:T(8,128)(2,1)} copy(bf16[64,8192]{1,0:T(8,128)(2,1)} %collective-permute-done.2) | data formatting | bytes 2097152 | tf_op jit(solution)/shard_map/ppermute | solution.py:23
  74.4 2.7 %copy.77 = bf16[64,8192]{0,1:T(8,128)(2,1)} copy(bf16[64,8192]{1,0:T(8,128)(2,1)} %collective-permute-done.6) | data formatting | bytes 2097152 | tf_op jit(solution)/shard_map/ppermute | solution.py:26
  77.1 2.8 %copy.71 = bf16[64,8192]{0,1:T(8,128)(2,1)} copy(bf16[64,8192]{1,0:T(8,128)(2,1)} %collective-permute-done.3) | data formatting | bytes 2097152 | tf_op jit(solution)/shard_map/ppermute | solution.py:23
  79.9 37.6 %concatenate.15 = bf16[1024,8192]{0,1:T(8,128)(2,1)} concatenate(bf16[64,8192]{0,1:T(8,128)(2,1)} %copy.71, bf16[64,8192]{0,1:T(8,128)(2,1)} %copy.72, bf16[64,8192]{0,1:T(8,128)(2,1)} %copy.73, bf16[64,8192]{0,1:T(8,128)(2,1)} %copy.74, bf16[64,8192]{0,1:T(8,128)(2,1)S(1)} %fusion.6, bf16[64,8192]{0,1:T(8,128)(2,1)} %copy.75, bf16[64,8192]{0,1:T(8,128)(2,1)} %copy.76, ...), dimensions={0} | concatenate | bytes 33554432 | tf_op jit(solution)/shard_map/jit(_roll_dynamic)/concatenate | solution.py:30
  117.5 9.5 %fusion.10 = bf16[512,256]{0,1:T(8,128)(2,1)S(1)} fusion(bf16[1024,8,2,128]{3,2,1,0:T(2,128)(2,1)} %bitcast.128, bf16[1024,8192]{0,1:T(8,128)(2,1)} %concatenate.15, s32[]{:T(128)S(6)} %select_n.21), kind=kOutput, calls=%fused_computation.15 | convolution fusion | flops 2147614720 | bytes 12845060 | tf_op jit(solution)/shard_map/dot_general | solution.py:94
  127.1 0.1 copy.111
  127.2 0.3 fusion.39
  127.5 0.1 fusion.19
  127.6 0.3 convolution_bitcast_fusion.1
  127.9 0.3 multiply_reduce_fusion
  128.3 0.2 fusion.21
  128.5 0.2 fusion.17
  128.7 11.1 %convolution_convert_fusion = bf16[8192,2,128]{2,0,1:T(8,128)(2,1)} fusion(bf16[1024,8192]{0,1:T(8,128)(2,1)} %concatenate.15, s32[]{:T(128)S(6)} %select_n.21, f32[640,1,1,128]{0,3,2,1:T(8,128)S(1)} %convolution_bitcast_fusion.1, f32[640,1,1,128]{0,3,2,1:T(8,128)S(1)} %fusion.17), kind=kOutput, calls=%fused_computation | convolution fusion | flops 2150105088 | bytes 13238276 | tf_op jit(solution)/shard_map/dot_general | solution.py:130
  139.8 0.0 reduce-scatter.5.cloned.1.call-start
  139.9 66.9 %reduce-scatter.3.cloned.1.call-done = bf16[1024,2,128]{2,0,1:T(8,128)(2,1)} async-done(((bf16[8192,2,128]{2,0,1:T(8,128)(2,1)}), bf16[1024,2,128]{2,0,1:T(8,128)(2,1)}) %reduce-scatter.3.cloned.1.call-update) | async-done | bytes 524304 | tf_op jit(solution)/shard_map/reduce_scatter | solution.py:36
  206.8 0.2 convolution_multiply_fusion.1
  207.0 30.8 %reduce-scatter.5.cloned.1.call-done = bf16[256,2,128]{2,0,1:T(8,128)(2,1)} async-done(((bf16[1024,2,128]{2,0,1:T(8,128)(2,1)}), bf16[256,2,128]{2,0,1:T(8,128)(2,1)}) %reduce-scatter.5.cloned.1.call-update) | async-done | bytes 131088 | tf_op jit(solution)/shard_map/reduce_scatter | solution.py:36
  237.8 1.6 broadcast_in_dim.24
  239.4 3.4 %all-to-all-start = ((bf16[2,256,2,128]{3,1,2,0:T(8,128)(2,1)}), bf16[2,256,2,128]{3,1,2,0:T(8,128)(2,1)S(1)}, u32[]{:S(2)}, u32[]{:S(2)}) async-start(bf16[2,256,2,128]{3,1,2,0:T(8,128)(2,1)} %broadcast_in_dim.24), calls=%async_computation.2 | async-start | bytes 524288 | tf_op jit(solution)/shard_map/all_to_all | solution.py:42
  242.9 0.8 copy.101
  243.7 0.8 copy.100
  244.4 0.3 convolution_convert_fusion.1
  244.7 0.7 copy.99
  245.5 2.6 %all-to-all-done = bf16[2,256,2,128]{3,1,2,0:T(8,128)(2,1)S(1)} async-done(((bf16[2,256,2,128]{3,1,2,0:T(8,128)(2,1)}), bf16[2,256,2,128]{3,1,2,0:T(8,128)(2,1)S(1)}, u32[]{:S(2)}, u32[]{:S(2)}) %all-to-all-start) | async-done | bytes 262176 | tf_op jit(solution)/shard_map/all_to_all | solution.py:42
  248.1 0.9 copy.102
  (34 shorter events, 0.2 us)
Async XLA Ops:
  7.2 4.2 %copy-start.4 = (f32[8192]{0:T(1024)S(1)}, f32[8192]{0:T(1024)}, u32[]{:S(2)}) copy-start(f32[8192]{0:T(1024)} %param.11) | copy-start | bytes 98308
  7.2 110.3 %all-gather.2.cloned.1.call-start = ((), (), s32[]{:S(2)}) async-start(), calls=%async_computation.3 | async-start | bytes 4325376 | tf_op jit(solution)/shard_map/all_gather | solution.py:92
  7.9 198.8 %reduce-scatter.3.cloned.1.call-start = ((), (), s32[]{:S(2)}) async-start(), calls=%async_computation.4 | async-start | bytes 4718592 | tf_op jit(solution)/shard_map/reduce_scatter | solution.py:36
  10.0 1.3 copy-start
  11.3 35.8 %copy-start.1 = (bf16[1,128,2,128]{3,2,1,0:T(2,128)(2,1)S(1)}, bf16[1,128,2,128]{3,2,1,0:T(2,128)(2,1)}, u32[]{:S(2)}) copy-start(bf16[1,128,2,128]{3,2,1,0:T(2,128)(2,1)} %param.14) | copy-start | bytes 196612
  11.3 35.8 %copy-start.2 = (bf16[1,128,256]{2,1,0:T(8,128)(2,1)S(1)}, bf16[1,128,256]{2,1,0:T(8,128)(2,1)}, u32[]{:S(2)}) copy-start(bf16[1,128,256]{2,1,0:T(8,128)(2,1)} %param.13) | copy-start | bytes 196612
  11.3 49.7 %copy-start.3 = (bf16[1,128,256]{2,1,0:T(8,128)(2,1)S(1)}, bf16[1,128,256]{2,1,0:T(8,128)(2,1)}, u32[]{:S(2)}) copy-start(bf16[1,128,256]{2,1,0:T(8,128)(2,1)} %param.15) | copy-start | bytes 196612
  11.3 49.9 %copy-start.5 = (s32[1,128]{1,0:T(1,128)S(1)}, s32[1,128]{1,0:T(1,128)}, u32[]{:S(2)}) copy-start(s32[1,128]{1,0:T(1,128)} %param.17) | copy-start | bytes 1540
  11.4 50.0 %copy-start.6 = (s32[1,512]{1,0:T(1,128)S(1)}, s32[1,512]{1,0:T(1,128)}, u32[]{:S(2)}) copy-start(s32[1,512]{1,0:T(1,128)} %param.16) | copy-start | bytes 6148
  17.7 14.4 %collective-permute-start = (bf16[64,8192]{1,0:T(8,128)(2,1)}, bf16[64,8192]{1,0:T(8,128)(2,1)S(1)}, u32[]{:S(2)}, u32[]{:S(2)}) collective-permute-start(bf16[64,8192]{1,0:T(8,128)(2,1)} %copy.69), channel_id=1, source_target_pairs={{0,1},{1,2},{2,3},{3,4},{4,5},{5,6},{6,7},{7,0},{8,9},{9,10},{10,1... | collective-permute-start | bytes 3145736 | tf_op jit(solution)/shard_map/ppermute | solution.py:23
  17.7 14.4 %collective-permute-start.4 = (bf16[64,8192]{1,0:T(8,128)(2,1)}, bf16[64,8192]{1,0:T(8,128)(2,1)}, u32[]{:S(2)}, u32[]{:S(2)}) collective-permute-start(bf16[64,8192]{1,0:T(8,128)(2,1)} %copy.69), channel_id=1, source_target_pairs={{0,7},{1,0},{2,1},{3,2},{4,3},{5,4},{6,5},{7,6},{8,15},{9,8},{10,9... | collective-permute-start | bytes 3145736 | tf_op jit(solution)/shard_map/ppermute | solution.py:26
  32.1 14.3 %collective-permute-start.1 = (bf16[64,8192]{1,0:T(8,128)(2,1)S(1)}, bf16[64,8192]{1,0:T(8,128)(2,1)}, u32[]{:S(2)}, u32[]{:S(2)}) collective-permute-start(bf16[64,8192]{1,0:T(8,128)(2,1)S(1)} %collective-permute-done), channel_id=1, source_target_pairs={{0,1},{1,2},{2,3},{3,4},{4,5},{5,6},{6,7},{7,0},{8,9},{9,10},{10,1... | collective-permute-start | bytes 3145736 | tf_op jit(solution)/shard_map/ppermute | solution.py:23
  32.1 15.8 %collective-permute-start.5 = (bf16[64,8192]{1,0:T(8,128)(2,1)}, bf16[64,8192]{1,0:T(8,128)(2,1)}, u32[]{:S(2)}, u32[]{:S(2)}) collective-permute-start(bf16[64,8192]{1,0:T(8,128)(2,1)} %collective-permute-done.4), channel_id=1, source_target_pairs={{0,7},{1,0},{2,1},{3,2},{4,3},{5,4},{6,5},{7,6},{8,15},{9,8},{10,9... | collective-permute-start | bytes 3145736 | tf_op jit(solution)/shard_map/ppermute | solution.py:26
  46.5 14.5 %collective-permute-start.2 = (bf16[64,8192]{1,0:T(8,128)(2,1)}, bf16[64,8192]{1,0:T(8,128)(2,1)}, u32[]{:S(2)}, u32[]{:S(2)}) collective-permute-start(bf16[64,8192]{1,0:T(8,128)(2,1)} %collective-permute-done.1), channel_id=1, source_target_pairs={{0,1},{1,2},{2,3},{3,4},{4,5},{5,6},{6,7},{7,0},{8,9},{9,10},{10,1... | collective-permute-start | bytes 3145736 | tf_op jit(solution)/shard_map/ppermute | solution.py:23
  47.9 26.4 %collective-permute-start.6 = (bf16[64,8192]{1,0:T(8,128)(2,1)}, bf16[64,8192]{1,0:T(8,128)(2,1)}, u32[]{:S(2)}, u32[]{:S(2)}) collective-permute-start(bf16[64,8192]{1,0:T(8,128)(2,1)} %collective-permute-done.5), channel_id=1, source_target_pairs={{0,7},{1,0},{2,1},{3,2},{4,3},{5,4},{6,5},{7,6},{8,15},{9,8},{10,9... | collective-permute-start | bytes 3145736 | tf_op jit(solution)/shard_map/ppermute | solution.py:26
  61.0 16.1 %collective-permute-start.3 = (bf16[64,8192]{1,0:T(8,128)(2,1)}, bf16[64,8192]{1,0:T(8,128)(2,1)}, u32[]{:S(2)}, u32[]{:S(2)}) collective-permute-start(bf16[64,8192]{1,0:T(8,128)(2,1)} %collective-permute-done.2), channel_id=1, source_target_pairs={{0,1},{1,2},{2,3},{3,4},{4,5},{5,6},{6,7},{7,0},{8,9},{9,10},{10,1... | collective-permute-start | bytes 3145736 | tf_op jit(solution)/shard_map/ppermute | solution.py:23
  139.8 98.0 %reduce-scatter.5.cloned.1.call-start = ((), (), s32[]{:S(2)}) async-start(), calls=%async_computation.5 | async-start | bytes 655360 | tf_op jit(solution)/shard_map/reduce_scatter | solution.py:36
  239.4 8.6 %all-to-all-start = ((bf16[2,256,2,128]{3,1,2,0:T(8,128)(2,1)}), bf16[2,256,2,128]{3,1,2,0:T(8,128)(2,1)S(1)}, u32[]{:S(2)}, u32[]{:S(2)}) async-start(bf16[2,256,2,128]{3,1,2,0:T(8,128)(2,1)} %broadcast_in_dim.24), calls=%async_computation.2 | async-start | bytes 524288 | tf_op jit(solution)/shard_map/all_to_all | solution.py:42
Sparse Core Ops, SparseCore 0:
  11.2 105.5 all-gather.1
  139.9 66.7 reduce-scatter.2
  209.6 28.1 reduce-scatter.4
